TPU v7x, 512 devices: a whole 4x8x8 slice. The times are simulated.
512 devices in a mesh: section: 16 (over x_hi, z), tp: 32 (over y, x_lo, core).
Axes of the slice: x: 4 (x_hi: 2, x_lo: 2; x = x_hi * 2 + x_lo), y: 8, z: 8, core: 2. Of those that a mesh axis runs over, the one named last changes fastest.
Arguments:
- resid: bfloat16 [512, 4608], P('tp', 'section'), may hold values from -40 to 40
- act: bfloat16 [512, 36864], P(None, 'tp'), may hold values from -6 to 6
- w_down: bfloat16 [36864, 4608], P('tp', 'section'), may hold values from -0.03125 to 0.03125
- gain: float32 [4608], P('section'), may hold values from 0.1 to 1.9
- embed: bfloat16 [4608, 131072], P(None, ('section', 'tp')), may hold values from -24 to 24
- targets: int32 [512], replicated, may hold values from 0 to 131071
Outputs:
- final_hidden: bfloat16 [512, 4608], P('tp', 'section')
- logprob: float32 [512], replicated
All inputs are finite; a program needn't handle non-finite values.
Results may differ from a plain program's by a relative error of at most 0.0014.
Values may be sent and summed in bfloat16 or wider, within the bound.
A program may use at most 64 MiB of HBM per device.

v0:
```python
import jax
import jax.numpy as jnp
from jax import lax
from jax.sharding import PartitionSpec as P


def body(resid, act, w_down, gain, embed, targets):
    summed = lax.psum_scatter(
        jnp.dot(act, w_down, preferred_element_type=jnp.float32),
        "tp",
        scatter_dimension=0,
        tiled=True,
    )
    mixed = resid.astype(jnp.float32) + summed
    local_sq = jnp.sum(mixed * mixed, axis=1)
    total_sq = lax.psum(local_sq, "section")
    width = mixed.shape[1] * lax.axis_size("section")
    scale = lax.rsqrt(total_sq / width + 1e-06)
    final_hidden = (mixed * scale[:, None] * gain[None, :]).astype(jnp.bfloat16)
    wide_rows = lax.all_gather(final_hidden, "section", axis=1, tiled=True)
    logits = jnp.dot(
        lax.all_gather(wide_rows, "tp", axis=0, tiled=True),
        embed,
        preferred_element_type=jnp.float32,
    )
    vocab_start = lax.axis_index(("section", "tp")) * embed.shape[1]
    places = jnp.arange(embed.shape[1], dtype=jnp.int32)[None, :] + vocab_start
    chosen = places == targets[:, None]
    local_target = jnp.sum(jnp.where(chosen, logits, jnp.zeros_like(logits)), axis=1)
    local_max = jnp.max(logits, axis=1)
    top = lax.pmax(local_max, ("section", "tp"))
    local_total = jnp.sum(jnp.exp(logits - top[:, None]), axis=1)
    total, target_logit = lax.psum((local_total, local_target), ("section", "tp"))
    logprob = target_logit - top - jnp.log(total)
    return (final_hidden, logprob)


def solution(mesh):
    return jax.shard_map(
        body,
        mesh=mesh,
        in_specs=(
            P("tp", "section"),
            P(None, "tp"),
            P("tp", "section"),
            P("section"),
            P(None, ("section", "tp")),
            P(),
        ),
        out_specs=(P("tp", "section"), P()),
        check_vma=False,
    )
```

profile of v0, /device:TPU:1, one launch (start us, length us, event | category | flops | bytes accessed | tf_op | source)
XLA Modules:
  0.0 483.6 jit_solution(3262023201774990345)
XLA Ops:
  7.2 0.0 copy-start
  7.2 0.0 copy-start.2
  7.2 0.0 copy-start.4
  7.2 0.0 reduce-scatter.2.cloned.1.call-start
  7.2 3.3 fusion.1
  10.5 0.0 reduce-scatter.2.cloned.1.call-update
  10.6 0.0 all-gather.3.cloned.1.call-start
  10.6 121.7 %reduce-scatter.2.cloned.1.call-done = f32[16,288]{1,0:T(8,128)} async-done(((f32[512,288]{1,0:T(8,128)}), f32[16,288]{1,0:T(8,128)}) %reduce-scatter.2.cloned.1.call-update) | async-done | bytes 18448 | tf_op jit(solution)/shard_map/reduce_scatter | solution.py:8
  132.3 0.9 multiply_reduce_fusion
  133.1 35.0 %psum.21 = f32[16]{0:T(128)S(1)} all-reduce(f32[16]{0:T(128)S(1)} %multiply_reduce_fusion), channel_id=1, replica_groups=mesh['section'=16,'tp'=32] {'section'}, use_global_device_ids=true, to_apply=%region_2.0 | all-reduce | flops 16 | bytes 128 | tf_op jit(solution)/shard_map/psum | solution.py:16
  168.2 0.8 multiply_convert_fusion
  169.0 29.6 %all-gather = bf16[16,288,16]{1,2,0:T(8,128)(2,1)S(1)} all-gather(bf16[1,288,16]{1,2,0:T(8,128)(2,1)S(1)} %bitcast.11), channel_id=1, replica_groups=mesh['section'=16,'tp'=32] {'section'}, dimensions={0}, use_global_device_ids=true | all-gather | bytes 156672 | tf_op jit(solution)/shard_map/all_gather | solution.py:20
  198.6 0.9 reshape.14
  199.5 0.0 all-gather.3.cloned.1.call-update
  199.6 0.0 copy-start.3
  199.6 80.8 %all-gather.3.cloned.1.call-done = bf16[512,4608]{1,0:T(8,128)(2,1)} async-done(((bf16[16,4608]{1,0:T(8,128)(2,1)}), bf16[512,4608]{1,0:T(8,128)(2,1)}) %all-gather.3.cloned.1.call-update) | async-done | bytes 4718608 | tf_op jit(solution)/shard_map/all_gather | solution.py:22
  280.4 0.0 copy-done
  280.4 3.8 fusion
  284.1 0.0 copy-done.1
  284.2 97.6 %pmax.7 = f32[512]{0:T(512)S(1)} all-reduce(f32[512]{0:T(512)S(1)} %get-tuple-element.6), channel_id=1, replica_groups=mesh['section'=16,'tp'=32] {'section','tp'}, use_global_device_ids=true, to_apply=%region_6.7 | all-reduce | flops 512 | bytes 4096 | tf_op jit(solution)/shard_map/pmax | solution.py:31
  381.8 0.0 copy-done.3
  381.8 0.1 select_reduce_fusion
  381.9 94.3 %all-reduce = (f32[512]{0:T(512)S(1)}, f32[512]{0:T(512)S(1)}) all-reduce(f32[512]{0:T(512)S(1)} %get-tuple-element.3, f32[512]{0:T(512)S(1)} %get-tuple-element.2), channel_id=1, replica_groups=mesh['section'=16,'tp'=32] {'section','tp'}, use_global_device_ids=true, to_apply=%region_8.9 | all-reduce | flops 1024 | bytes 8192 | tf_op jit(solution)/shard_map/psum | solution.py:33
  476.2 0.6 log_subtract_fusion
  (6 shorter events, 0.1 us)
Async XLA Ops:
  7.2 273.2 %copy-start = (bf16[4608,256]{1,0:T(8,128)(2,1)S(1)}, bf16[4608,256]{1,0:T(8,128)(2,1)}, u32[]{:S(2)}) copy-start(bf16[4608,256]{1,0:T(8,128)(2,1)} %param.10) | copy-start | bytes 7077892
  7.2 125.1 %copy-start.2 = (bf16[16,288]{1,0:T(8,128)(2,1)S(1)}, bf16[16,288]{1,0:T(8,128)(2,1)}, u32[]{:S(2)}) copy-start(bf16[16,288]{1,0:T(8,128)(2,1)} %param.6) | copy-start | bytes 27652
  7.2 161.0 %copy-start.4 = (f32[288]{0:T(512)S(1)}, f32[288]{0:T(512)}, u32[]{:S(2)}) copy-start(f32[288]{0:T(512)} %param.9) | copy-start | bytes 3460
  7.2 125.1 %reduce-scatter.2.cloned.1.call-start = ((), (), s32[]{:S(2)}) async-start(), calls=%async_computation.1 | async-start | bytes 811008 | tf_op jit(solution)/shard_map/reduce_scatter | solution.py:8
  10.6 269.8 %all-gather.3.cloned.1.call-start = ((), (), s32[]{:S(2)}) async-start(), calls=%async_computation.2 | async-start | bytes 4866048 | tf_op jit(solution)/shard_map/all_gather | solution.py:22
  169.0 115.2 %copy-start.1 = (bf16[16,288]{1,0:T(8,128)(2,1)}, bf16[16,288]{1,0:T(8,128)(2,1)S(1)}, u32[]{:S(2)}) copy-start(bf16[16,288]{1,0:T(8,128)(2,1)S(1)} %multiply_convert_fusion) | copy-start | bytes 27652
  199.6 182.2 %copy-start.3 = (s32[512]{0:T(512)S(1)}, s32[512]{0:T(512)}, u32[]{:S(2)}) copy-start(s32[512]{0:T(512)} %param.11) | copy-start | bytes 6148
Sparse Core Ops, SparseCore 0:
  10.8 121.4 reduce-scatter.1
  199.7 80.6 all-gather.2
where the time goes:
time: 484 us
  blocking collectives  257 us (53%)
  waiting for transfers between devices  203 us (42%)
  between operations  14.1 us (3%)
  matrix products  7.06 us (1%)
    reduce_scatter x1, waiting for transfers between devices, body(): lax.psum_scatter(jnp.dot(act, w_down, preferred_element_type=jnp.float32)...  122 us
    pmax x1, blocking collectives, body(): top = lax.pmax(local_max, ('section', 'tp'))  97.6 us
    psum x1, blocking collectives, body(): lax.psum((local_total, local_target), ('section', 'tp'))  94.3 us
    all_gather x1, waiting for transfers between devices, body(): lax.all_gather(wide_rows, 'tp', axis=0, tiled=True)  80.8 us
    psum x1, blocking collectives, body(): total_sq = lax.psum(local_sq, 'section')  35 us
    all_gather x1, blocking collectives, body(): wide_rows = lax.all_gather(final_hidden, 'section', axis=1, tiled=True)  29.6 us
  transfers between devices with their start and end apart: 2, of which 2 were waited for; matrix products, arithmetic and copies ran while one was open for 0% of the time, Pallas kernels for 0%

commit v1 on v0

v1 whole, which is shorter than its diff:
```python
import jax
import jax.numpy as jnp
from jax import lax
from jax.experimental import pallas as pl
from jax.experimental.pallas import tpu as pltpu
from jax.sharding import PartitionSpec as P

MESH = pl.DeviceIdType.MESH
F32 = jnp.float32
BF16 = jnp.bfloat16
HID, WID = 1152, 288
D_ALL = 4608
PADW = 384
COLS = 256


def send(src, dst, s_sem, r_sem, dev):
    return pltpu.make_async_remote_copy(
        src_ref=src, dst_ref=dst, send_sem=s_sem, recv_sem=r_sem, device_id=dev, device_id_type=MESH
    )


def kernel(
    act, w_down, resid, gain, embed, targets,
    fh_out, lp_out,
    a_buf, w_buf, r_in, g_in, t_in, e_buf,
    p_out, p_in, p_own, s_buf, s_in, m_buf, h_buf, scale_buf, acc,
    st1, st2, res,
    ld_sem, core_s, core_r, rs_s, rs_r, pl_s, pl_r, ring_s, ring_r, s1_s, s1_r, s2_s, s2_r,
):
    sec = lax.axis_index("section")
    tp = lax.axis_index("tp")
    core = lax.rem(tp, 2)
    xl = lax.rem(tp // 2, 2)
    y = tp // 4
    xh = sec // 8
    z = lax.rem(sec, 8)
    x = 2 * xh + xl
    first = core == 0
    u = jnp.where(first, y, z)
    w = jnp.where(first, z, y)

    def dev(x2, y2, z2, c2):
        return ((x2 // 2) * 8 + z2, (y2 * 2 + lax.rem(x2, 2)) * 2 + c2)

    sibling = dev(x, y, z, 1 - core)

    def rs_peer(i):
        return lax.rem(y + i // 2, 8), lax.rem(xl + i, 2)

    def rs_dev(i):
        y2, xl2 = rs_peer(i)
        return dev(2 * xh + xl2, y2, z, core)

    def grid_dev(x2, u2, w2):
        return dev(x2, jnp.where(first, u2, w2), jnp.where(first, w2, u2), core)

    def plane_dev(i):
        return grid_dev(lax.rem(x + i // 8, 4), lax.rem(u + i, 8), w)

    def line_dev(i):
        return grid_dev(x, u, lax.rem(w + i, 8))

    def load(src, dst, k):
        return pltpu.make_async_copy(src, dst, ld_sem.at[k])

    l_w = load(w_down, w_buf, 0)
    l_a0 = load(act.at[:, 1 - core], a_buf.at[0], 1)
    l_a1 = load(act.at[:, core], a_buf.at[1], 2)
    l_r = load(resid, r_in, 3)
    l_g = load(gain, g_in, 4)
    l_t = load(targets.at[core], t_in, 5)
    l_e = load(embed, e_buf.at[core, :, pl.ds(0, WID), :], 6)
    for l in (l_w, l_a0, l_a1, l_r, l_g, l_t, l_e):
        l.start()

    barrier = pltpu.get_barrier_semaphore()
    pl.semaphore_signal(barrier, inc=1, device_id=sibling, device_id_type=MESH)

    def sig(peer):
        def go(i, carry):
            pl.semaphore_signal(barrier, inc=1, device_id=peer(i), device_id_type=MESH)
            return carry
        return go

    lax.fori_loop(1, 16, sig(rs_dev), 0)
    lax.fori_loop(1, 32, sig(plane_dev), 0)
    lax.fori_loop(1, 8, sig(line_dev), 0)

    def zero(s, carry):
        for c in range(2):
            e_buf[c, s, pl.ds(WID, PADW - WID), :] = jnp.zeros((PADW - WID, COLS), BF16)
        return carry

    lax.fori_loop(0, 16, zero, 0)
    p_out[:, pl.ds(256, 128)] = jnp.zeros((256, 128), F32)
    p_own[:, pl.ds(256, 128)] = jnp.zeros((256, 128), F32)

    def partial(k):
        return lax.dot_general(
            a_buf[k].reshape(256, HID), w_buf[...], (((1,), (1,)), ((), ())), preferred_element_type=F32
        )

    l_w.wait()
    l_a0.wait()
    p_out[:, pl.ds(0, WID)] = partial(0)
    pl.semaphore_wait(barrier, 1 + 15 + 31 + 7)
    c_pair = send(p_out, p_in, core_s.at[0], core_r.at[0], sibling)
    c_pair.start()
    l_a1.wait()
    p_own[:, pl.ds(0, WID)] = partial(1)
    c_pair.wait_recv()
    for b in range(16):
        rows = pl.ds(16 * b, 16)
        v = p_own[rows, :] + p_in[rows, :]
        s_buf[b, 0] = v[0:8, 0:128]
        s_buf[b, 1] = v[0:8, 128:256]
        s_buf[b, 2] = v[8:16, 0:128]
        s_buf[b, 3] = v[8:16, 128:256]
        s_buf[b, 4] = v[0:8, 256:384] + pltpu.roll(v[8:16, 256:384], 32, 1)

    def rs_copy(i):
        y2, xl2 = rs_peer(i)
        return send(s_buf.at[y2 * 2 + xl2], s_in.at[i], rs_s.at[i], rs_r.at[i], rs_dev(i))

    def rs_start(i, carry):
        rs_copy(i).start()
        return carry

    lax.fori_loop(1, 16, rs_start, 0)

    l_e.wait()
    c_emb = send(
        e_buf.at[core, :, pl.ds(0, WID), :], e_buf.at[core, :, pl.ds(0, WID), :],
        core_s.at[1], core_r.at[1], sibling,
    )
    c_emb.start()
    l_r.wait()
    l_g.wait()
    l_t.wait()

    def rs_wait(i, carry):
        rs_copy(i).wait_recv()
        return carry

    lax.fori_loop(1, 16, rs_wait, 0)
    total = s_buf[y * 2 + xl]
    for i in range(1, 16):
        total = total + s_in[i]
    lane8 = lax.broadcasted_iota(jnp.int32, (8, 128), 1)
    m_buf[0:8, 0:128] = total[0]
    m_buf[0:8, 128:256] = total[1]
    m_buf[8:16, 0:128] = total[2]
    m_buf[8:16, 128:256] = total[3]
    m_buf[0:8, 256:384] = jnp.where(lane8 < 32, total[4], 0.0)
    m_buf[8:16, 256:384] = jnp.where(lane8 < 32, pltpu.roll(total[4], 96, 1), 0.0)
    mixed = m_buf[:, pl.ds(0, WID)] + r_in[...].astype(F32)
    m_buf[:, pl.ds(0, WID)] = mixed
    sq = jnp.sum(mixed * mixed, axis=1, keepdims=True)
    sq_hi = sq.astype(BF16).astype(F32)
    sq_rest = sq - sq_hi
    sq_mid = sq_rest.astype(BF16).astype(F32)
    sq_lo = (sq_rest - sq_mid).astype(BF16).astype(F32)
    m_own = h_buf.at[w, x * 8 + u]
    lane = lax.broadcasted_iota(jnp.int32, (16, 128), 1)
    tail = jnp.where(lane == 32, sq_hi, jnp.where(lane == 33, sq_mid, jnp.where(lane == 34, sq_lo, 0.0)))
    m_own[:, pl.ds(256, 128)] = tail.astype(BF16)
    m_own[:, pl.ds(0, WID)] = (mixed * g_in[...]).astype(BF16)

    def pl_copy(i):
        return send(h_buf.at[w, x * 8 + u], h_buf.at[w, x * 8 + u], pl_s.at[i], pl_r.at[i], plane_dev(i))

    def pl_start(i, carry):
        pl_copy(i).start()
        return carry

    def pl_wait(i, carry):
        pl_copy(i).wait_recv()
        return carry

    lax.fori_loop(1, 32, pl_start, 0)
    lax.fori_loop(1, 32, pl_wait, 0)

    right, left = line_dev(1), line_dev(7)

    def ring_copy(way, k, c):
        at = lax.rem(w + (8 - (k - 1) if way == 0 else k - 1), 8)
        part = h_buf.at[at, pl.ds(16 * c, 16)]
        j = (way * 4 + k - 1) * 2 + c
        return send(part, part, ring_s.at[j], ring_r.at[j], right if way == 0 else left)

    hops = {(0, 0): 4, (0, 1): 3, (1, 0): 3, (1, 1): 4}
    sent = []
    for k in range(1, 6):
        for c in range(2):
            for way in range(2):
                if 2 <= k <= hops[way, c] + 1:
                    ring_copy(way, k - 1, c).wait_recv()
                if k <= hops[way, c]:
                    cp = ring_copy(way, k, c)
                    cp.start()
                    sent.append(cp)
    c_emb.wait_recv()

    sel = (lane >= 32) & (lane < 35)

    def slot(y2, x2, z2):
        return jnp.where(first, z2, y2), x2 * 8 + jnp.where(first, y2, z2)

    def norm(b, carry):
        y2, xl2 = b // 2, lax.rem(b, 2)
        t = jnp.zeros((16, 128), F32)
        for s in range(16):
            w2, p2 = slot(y2, 2 * (s // 8) + xl2, s % 8)
            t = t + h_buf[w2, p2, :, pl.ds(256, 128)].astype(F32)
        t = jnp.sum(jnp.where(sel, t, 0.0), axis=1, keepdims=True)
        scale_buf[pl.ds(pl.multiple_of(16 * b, 16), 16), :] = jnp.broadcast_to(
            lax.rsqrt(t / D_ALL + 1e-06), (16, 128)
        )
        return carry

    lax.fori_loop(0, 16, norm, 0)
    own_scale = scale_buf[pl.ds(pl.multiple_of(16 * (2 * y + xl), 16), 16), pl.ds(0, 1)]
    fh_out[...] = (m_buf[:, pl.ds(0, WID)] * own_scale * g_in[...]).astype(BF16)

    acc[...] = jnp.zeros_like(acc)

    def logits(s, carry):
        parts = []
        for b in range(16):
            w2, p2 = slot(b // 2, 2 * (s // 8) + b % 2, lax.rem(s, 8))
            parts.append(h_buf[w2, p2])
        lhs = jnp.concatenate(parts, axis=0)
        for c in range(2):
            acc[c] += jnp.dot(lhs, e_buf[c, s], preferred_element_type=F32)
        return carry

    lax.fori_loop(0, 16, logits, 0)
    scale = scale_buf[:, pl.ds(0, 1)]
    lt = jnp.concatenate([(acc[c] * scale).T for c in range(2)], axis=0)
    top = jnp.max(lt, axis=0, keepdims=True)
    lse = top + jnp.log(jnp.sum(jnp.exp(lt - top), axis=0, keepdims=True))
    ids = lax.broadcasted_iota(jnp.int32, (2 * COLS, 256), 0) + (sec * 32 + tp - core) * COLS
    tgt = jnp.sum(jnp.where(ids == t_in[...], lt, 0.0), axis=0, keepdims=True)

    def put(ref, lse, tgt):
        ref[0:1, :] = lse[:, 0:128]
        ref[1:2, :] = lse[:, 128:256]
        ref[2:3, :] = tgt[:, 0:128]
        ref[3:4, :] = tgt[:, 128:256]

    def merge(ref, n):
        ls = ref[:, 0:2, :]
        top = jnp.max(ls, axis=0)
        return top + jnp.log(jnp.sum(jnp.exp(ls - top[None]), axis=0)), jnp.sum(ref[:, 2:4, :], axis=0)

    put(st1.at[w], lse, tgt)

    def s1_copy(i):
        return send(st1.at[w], st1.at[w], s1_s.at[i], s1_r.at[i], line_dev(i))

    def s2_copy(i):
        return send(st2.at[x * 8 + u], st2.at[x * 8 + u], s2_s.at[i], s2_r.at[i], plane_dev(i))

    def starter(copy):
        def go(i, carry):
            copy(i).start()
            return carry
        return go

    def waiter(copy):
        def go(i, carry):
            copy(i).wait_recv()
            return carry
        return go

    def ender(copy):
        def go(i, carry):
            copy(i).wait_send()
            return carry
        return go

    lax.fori_loop(1, 8, starter(s1_copy), 0)
    lax.fori_loop(1, 8, waiter(s1_copy), 0)
    ls1, tg1 = merge(st1, 8)
    st2[x * 8 + u, 0:2, :] = ls1
    st2[x * 8 + u, 2:4, :] = tg1
    lax.fori_loop(1, 32, starter(s2_copy), 0)
    lax.fori_loop(1, 32, waiter(s2_copy), 0)
    ls2, tg2 = merge(st2, 32)
    res[core] = tg2 - ls2
    c_res = send(res.at[core], res.at[core], core_s.at[2], core_r.at[2], sibling)
    c_res.start()

    c_pair.wait_send()
    c_emb.wait_send()
    lax.fori_loop(1, 16, ender(rs_copy), 0)
    lax.fori_loop(1, 32, ender(pl_copy), 0)
    for cp in sent:
        cp.wait_send()
    lax.fori_loop(1, 8, ender(s1_copy), 0)
    lax.fori_loop(1, 32, ender(s2_copy), 0)
    c_res.wait()
    lp_out[...] = res[...]


def body(resid, act, w_down, gain, embed, targets):
    anyspec = pl.BlockSpec(memory_space=pl.ANY)
    vmem = pl.BlockSpec(memory_space=pltpu.VMEM)
    dma = pltpu.SemaphoreType.DMA
    fh, lp = pl.pallas_call(
        kernel,
        out_shape=(
            jax.ShapeDtypeStruct((16, WID), BF16),
            jax.ShapeDtypeStruct((2, 2, 128), F32),
        ),
        in_specs=[anyspec] * 6,
        out_specs=(vmem, vmem),
        scratch_shapes=[
            pltpu.VMEM((2, 16, 16, HID), BF16),
            pltpu.VMEM((WID, HID), BF16),
            pltpu.VMEM((16, WID), BF16),
            pltpu.VMEM((1, WID), F32),
            pltpu.VMEM((1, 256), jnp.int32),
            pltpu.VMEM((2, 16, PADW, COLS), BF16),
            pltpu.VMEM((256, PADW), F32),
            pltpu.VMEM((256, PADW), F32),
            pltpu.VMEM((256, PADW), F32),
            pltpu.VMEM((16, 5, 8, 128), F32),
            pltpu.VMEM((16, 5, 8, 128), F32),
            pltpu.VMEM((16, PADW), F32),
            pltpu.VMEM((8, 32, 16, PADW), BF16),
            pltpu.VMEM((256, 128), F32),
            pltpu.VMEM((2, 256, COLS), F32),
            pltpu.VMEM((8, 4, 128), F32),
            pltpu.VMEM((32, 4, 128), F32),
            pltpu.VMEM((2, 2, 128), F32),
            dma((7,)), dma((3,)), dma((3,)), dma((16,)), dma((16,)), dma((32,)), dma((32,)),
            dma((16,)), dma((16,)), dma((8,)), dma((8,)), dma((32,)), dma((32,)),
        ],
        compiler_params=pltpu.CompilerParams(
            collective_id=0, has_side_effects=True, vmem_limit_bytes=40 << 20
        ),
        name="ffn_vocab",
    )(
        act.reshape(16, 2, 16, HID),
        w_down.T,
        resid,
        gain.reshape(1, WID),
        embed.reshape(16, WID, COLS),
        targets.reshape(16, 2, 16).transpose(1, 0, 2).reshape(2, 1, 256),
    )
    logprob = lp.reshape(2, 16, 16).transpose(1, 0, 2).reshape(512)
    return fh, logprob


def solution(mesh):
    return jax.shard_map(
        body,
        mesh=mesh,
        in_specs=(
            P("tp", "section"),
            P(None, "tp"),
            P("tp", "section"),
            P("section"),
            P(None, ("section", "tp")),
            P(),
        ),
        out_specs=(P("tp", "section"), P()),
        check_vma=False,
    )
```

time: 484 us -> 90 us (0.19)
  blocking collectives: 257 us -> 0 us
  waiting for transfers between devices: 203 us -> 0 us
  Pallas kernels: 0 us -> 81.3 us
  between operations: 14.1 us -> 0.66 us
  matrix products: 7.06 us -> 0 us
  local copies, waits for them, and re-layouts: 0.95 us -> 7.63 us
    psum x2 -> x0, blocking collectives: 129 us -> none  [the longest x1 94.3 us: body(): lax.psum((local_total, local_target), ('section', 'tp'))]
    reduce_scatter x1 -> x0, waiting for transfers between devices: 122 us -> none  [body(): lax.psum_scatter(jnp.dot(act, w_down, preferred_element_type=jnp.float32)...]
    pmax x1 -> x0, blocking collectives: 97.6 us -> none  [body(): top = lax.pmax(local_max, ('section', 'tp'))]
    pallas_call x0 -> x1, Pallas kernels: none -> 81.3 us  [body(): pl.pallas_call(kernel, out_shape=(jax.ShapeDtypeStruct((16, WID), BF16),...]
    all_gather x1 -> x0, waiting for transfers between devices: 80.8 us -> none  [body(): lax.all_gather(wide_rows, 'tp', axis=0, tiled=True)]
    all_gather x1 -> x0, blocking collectives: 29.6 us -> none  [body(): wide_rows = lax.all_gather(final_hidden, 'section', axis=1, tiled=True)]
    dot_general x2 -> x0, matrix products: 7.06 us -> none  [the longest x1 3.78 us: body(): jnp.dot(lax.all_gather(wide_rows, 'tp', axis=0, tiled=True), embed, prefe...]
  transfers between devices with their start and end apart: 2 -> 0, of which waited for: 2 -> 0; matrix products, arithmetic and copies ran while one was open for 0% -> 0% of each run, Pallas kernels for 0% -> 0%
where the time goes in v1:
time: 90 us; the launch traced here: 89.6 us
  Pallas kernels  81.3 us (90%)
  local copies, waits for them, and re-layouts  7.63 us (8%)
    pallas_call x1, Pallas kernels, body(): pl.pallas_call(kernel, out_shape=(jax.ShapeDtypeStruct((16, WID), BF16),...  81.3 us
    unnamed x9, local copies, waits for them, and re-layouts  5.33 us

profile of v1, /device:TPU:1, one launch (start us, length us, event | category | flops | bytes accessed | tf_op | source)
XLA Modules:
  0.0 89.6 jit_solution(2508474647102921037)
XLA Ops:
  0.6 0.7 reshape.26.gain
  1.3 0.8 reshape.28
  2.1 0.1 reshape.29.targets
  2.2 0.0 copy-start
  2.2 1.7 %copy-done = bf16[4608,256]{1,0:T(8,128)(2,1)S(1)} copy-done((bf16[4608,256]{1,0:T(8,128)(2,1)S(1)}, bf16[4608,256]{1,0:T(8,128)(2,1)}, u32[]{:S(2)}) %copy-start) | copy-done | bytes 2359320
  3.8 0.0 copy-start.1
  3.8 1.3 %copy-done.1 = bf16[512,1152]{1,0:T(8,128)(2,1)S(1)} copy-done((bf16[512,1152]{1,0:T(8,128)(2,1)S(1)}, bf16[512,1152]{1,0:T(8,128)(2,1)}, u32[]{:S(2)}) %copy-start.1) | copy-done | bytes 1179672
  5.1 0.0 copy-start.2
  5.1 1.1 %copy-done.2 = bf16[1152,288]{0,1:T(8,128)(2,1)S(1)} copy-done((bf16[1152,288]{0,1:T(8,128)(2,1)S(1)}, bf16[1152,288]{0,1:T(8,128)(2,1)}, u32[]{:S(2)}) %copy-start.2) | copy-done | bytes 663576
  6.2 0.0 copy-start.3
  6.2 0.7 copy-done.3
  6.9 81.3 %ffn_vocab.1 = (bf16[16,288]{1,0:T(8,128)(2,1)S(1)}, f32[2,2,128]{2,1,0:T(2,128)S(1)}) custom-call(bf16[16,2,16,1152]{3,2,1,0:T(8,128)(2,1)S(1)} %bitcast.8, bf16[288,1152]{1,0:T(8,128)(2,1)S(1)} %bitcast.9, bf16[16,288]{1,0:T(8,128)(2,1)S(1)} %copy-done.3, f32[1,288]{1,0:T(1,128)S(1)} %reshape.26.gain, bf16[16,288,256]{2,1,0:T(8,128)(2,1)S(1)} %bitcast.7, ...), custom_call_target="tpu_custom_call" | custom-call | tf_op jit(solution)/shard_map/ffn_vocab/pallas_call | solution.py:311
  88.3 0.1 reshape.30
  88.4 0.7 reshape.31
  89.0 0.6 copy.13
  (2 shorter events, 0.0 us)
Async XLA Ops:
  2.2 1.7 %copy-start = (bf16[4608,256]{1,0:T(8,128)(2,1)S(1)}, bf16[4608,256]{1,0:T(8,128)(2,1)}, u32[]{:S(2)}) copy-start(bf16[4608,256]{1,0:T(8,128)(2,1)} %param.10) | copy-start | bytes 7077892
  3.8 1.3 %copy-start.1 = (bf16[512,1152]{1,0:T(8,128)(2,1)S(1)}, bf16[512,1152]{1,0:T(8,128)(2,1)}, u32[]{:S(2)}) copy-start(bf16[512,1152]{1,0:T(8,128)(2,1)} %param.7) | copy-start | bytes 3538948
  5.1 1.1 %copy-start.2 = (bf16[1152,288]{0,1:T(8,128)(2,1)S(1)}, bf16[1152,288]{0,1:T(8,128)(2,1)}, u32[]{:S(2)}) copy-start(bf16[1152,288]{0,1:T(8,128)(2,1)} %param.8) | copy-start | bytes 1990660
  6.2 0.7 copy-start.3

commit v2 on v1

v2 whole, which is shorter than its diff:
```python
import jax
import jax.numpy as jnp
from jax import lax
from jax.experimental import pallas as pl
from jax.experimental.pallas import tpu as pltpu
from jax.sharding import PartitionSpec as P

MESH = pl.DeviceIdType.MESH
F32 = jnp.float32
BF16 = jnp.bfloat16
HID, WID = 1152, 288
D_ALL = 4608
PADW = 384
COLS = 256


def send(src, dst, s_sem, r_sem, dev):
    return pltpu.make_async_remote_copy(
        src_ref=src, dst_ref=dst, send_sem=s_sem, recv_sem=r_sem, device_id=dev, device_id_type=MESH
    )


def kernel(
    act, w_down, resid, gain, embed, targets,
    fh_out, lp_out,
    a_buf, w_buf, r_in, g_in, t_in, e0, e1, e2,
    p_out, p_in, p_own, s_buf, s_in, m_buf, hx, hw, ht, lt_buf, scale_buf, acc,
    st1, st2, res,
    ld_sem, core_s, core_r, rs_s, rs_r, xp_s, xp_r, wp_s, wp_r, xl_s, xl_r, wl_s, wl_r, s1_s, s1_r, s2_s, s2_r,
):
    sec = lax.axis_index("section")
    tp = lax.axis_index("tp")
    core = lax.rem(tp, 2)
    xl = lax.rem(tp // 2, 2)
    y = tp // 4
    xh = sec // 8
    z = lax.rem(sec, 8)
    x = 2 * xh + xl
    first = core == 0
    u = jnp.where(first, y, z)
    w = jnp.where(first, z, y)

    def dev(x2, y2, z2, c2):
        return ((x2 // 2) * 8 + z2, (y2 * 2 + lax.rem(x2, 2)) * 2 + c2)

    sibling = dev(x, y, z, 1 - core)

    def rs_peer(i):
        return lax.rem(y + i // 2, 8), lax.rem(xl + i, 2)

    def rs_dev(i):
        y2, xl2 = rs_peer(i)
        return dev(2 * xh + xl2, y2, z, core)

    def grid_dev(x2, u2, w2):
        return dev(x2, jnp.where(first, u2, w2), jnp.where(first, w2, u2), core)

    def plane_dev(i):
        return grid_dev(lax.rem(x + i // 8, 4), lax.rem(u + i, 8), w)

    def yz_dev(i):
        return dev(x, lax.rem(y + i // 8, 8), lax.rem(z + i, 8), core)

    def x_dev(k):
        return dev(2 * lax.rem(xh + k // 2, 2) + lax.rem(xl + k, 2), y, z, core)

    def line_dev(i):
        return grid_dev(x, u, lax.rem(w + i, 8))

    def load(src, dst, k):
        return pltpu.make_async_copy(src, dst, ld_sem.at[k])

    l_w = load(w_down, w_buf, 0)
    l_a0 = load(act.at[:, 1 - core], a_buf.at[0], 1)
    l_a1 = load(act.at[:, core], a_buf.at[1], 2)
    l_r = load(resid, r_in, 3)
    l_g = load(gain, g_in, 4)
    l_t = load(targets, t_in, 5)
    l_e = load(embed.at[:, pl.ds(0, 128)], e0.at[core], 6)
    l_f = load(embed.at[:, pl.ds(128, 128)], e1.at[core], 7)
    l_h = load(embed.at[:, pl.ds(256, 32)], e2.at[core], 8)
    for l in (l_w, l_a0, l_a1, l_r, l_g, l_t, l_e, l_f, l_h):
        l.start()

    barrier = pltpu.get_barrier_semaphore()
    pl.semaphore_signal(barrier, inc=1, device_id=sibling, device_id_type=MESH)

    def sig(peer):
        def go(i, carry):
            pl.semaphore_signal(barrier, inc=1, device_id=peer(i), device_id_type=MESH)
            return carry
        return go

    lax.fori_loop(0, 8, sig(lambda i: rs_dev(2 * i + 1)), 0)
    lax.fori_loop(1, 64, sig(yz_dev), 0)
    lax.fori_loop(8, 32, sig(plane_dev), 0)

    p_out[:, pl.ds(256, 128)] = jnp.zeros((256, 128), F32)
    p_own[:, pl.ds(256, 128)] = jnp.zeros((256, 128), F32)

    def partial(k):
        return lax.dot_general(
            a_buf[k].reshape(256, HID), w_buf[...], (((1,), (1,)), ((), ())), preferred_element_type=F32
        )

    l_w.wait()
    l_a0.wait()
    p_out[:, pl.ds(0, WID)] = partial(0)
    pl.semaphore_wait(barrier, 1 + 8 + 63 + 24)
    c_pair = send(p_out, p_in, core_s.at[0], core_r.at[0], sibling)
    c_pair.start()
    l_a1.wait()
    p_own[:, pl.ds(0, WID)] = partial(1)
    c_pair.wait_recv()
    for b in range(16):
        rows = pl.ds(16 * b, 16)
        v = p_own[rows, :] + p_in[rows, :]
        s_buf[b, 0] = v[0:8, 0:128]
        s_buf[b, 1] = v[0:8, 128:256]
        s_buf[b, 2] = v[8:16, 0:128]
        s_buf[b, 3] = v[8:16, 128:256]
        s_buf[b, 4] = v[0:8, 256:384] + pltpu.roll(v[8:16, 256:384], 32, 1)

    def rs_copy(i):
        y2, xl2 = rs_peer(i)
        return send(s_buf.at[y2 * 2 + xl2], s_in.at[i], rs_s.at[i], rs_r.at[i], rs_dev(i))

    def rs_start(i, carry):
        rs_copy(i).start()
        return carry

    lax.fori_loop(1, 16, rs_start, 0)

    l_e.wait()
    l_f.wait()
    l_h.wait()
    c_emb = [
        send(e.at[core], e.at[core], core_s.at[k], core_r.at[k], sibling)
        for k, e in ((1, e0), (2, e1), (3, e2))
    ]
    for cp in c_emb:
        cp.start()
    l_r.wait()
    l_g.wait()
    l_t.wait()

    def rs_wait(i, carry):
        rs_copy(i).wait_recv()
        return carry

    lax.fori_loop(1, 16, rs_wait, 0)
    total = s_buf[y * 2 + xl]
    for i in range(1, 16):
        total = total + s_in[i]
    lane8 = lax.broadcasted_iota(jnp.int32, (8, 128), 1)
    m_buf[0:8, 0:128] = total[0]
    m_buf[0:8, 128:256] = total[1]
    m_buf[8:16, 0:128] = total[2]
    m_buf[8:16, 128:256] = total[3]
    m_buf[0:8, 256:384] = jnp.where(lane8 < 32, total[4], 0.0)
    m_buf[8:16, 256:384] = jnp.where(lane8 < 32, pltpu.roll(total[4], 96, 1), 0.0)
    g_row = g_in[...].reshape(1, WID)
    mixed = m_buf[:, pl.ds(0, WID)] + r_in[...].astype(F32)
    m_buf[:, pl.ds(0, WID)] = mixed
    sq = jnp.sum(mixed * mixed, axis=1, keepdims=True)
    sq_hi = sq.astype(BF16).astype(F32)
    sq_rest = sq - sq_hi
    sq_mid = sq_rest.astype(BF16).astype(F32)
    sq_lo = (sq_rest - sq_mid).astype(BF16).astype(F32)
    lane = lax.broadcasted_iota(jnp.int32, (16, 128), 1)
    tail = jnp.where(lane == 32, sq_hi, jnp.where(lane == 33, sq_mid, jnp.where(lane == 34, sq_lo, 0.0)))
    piece = (mixed * g_row).astype(BF16)
    w_own = hw.at[w, x * 8 + u]
    w_own[:, pl.ds(128, 128)] = tail.astype(BF16)
    w_own[:, pl.ds(0, 160)] = piece[:, 128:288]
    hx[x, z * 8 + y] = piece[:, 0:128]

    def starter(copy):
        def go(i, carry):
            copy(i).start()
            return carry
        return go

    def waiter(copy):
        def go(i, carry):
            copy(i).wait_recv()
            return carry
        return go

    def ender(copy):
        def go(i, carry):
            copy(i).wait_send()
            return carry
        return go

    def wp_copy(i):
        at = hw.at[w, x * 8 + u]
        return send(at, at, wp_s.at[i], wp_r.at[i], plane_dev(i))

    def xp_copy(i):
        at = hx.at[x, z * 8 + y]
        return send(at, at, xp_s.at[i], xp_r.at[i], yz_dev(i))

    def x_copy(k, z2):
        block = hx.at[x, pl.ds(pl.multiple_of(z2 * 8, 8), 8)]
        return send(block, block, xl_s.at[k * 8 + z2], xl_r.at[k * 8 + z2], x_dev(k))

    def x_forward(dz):
        def go(i, carry):
            xp_copy(8 * i + dz).wait_recv()
            return carry
        lax.fori_loop(0 if dz else 1, 8, go, 0)
        z2 = lax.rem(z + 8 - dz, 8)
        for k in (1, 2, 3):
            x_copy(k, z2).start()

    lax.fori_loop(1, 32, starter(wp_copy), 0)
    for dz in (0, 1, 7, 2, 6, 3, 5, 4):
        def go(i, carry, dz=dz):
            xp_copy(8 * i + dz).start()
            return carry
        lax.fori_loop(0 if dz else 1, 8, go, 0)
    for dz in (0, 1, 7):
        x_forward(dz)
    lax.fori_loop(1, 32, waiter(wp_copy), 0)

    for c in range(2):
        squares = jnp.zeros((16, 128), F32)
        for j in range(4):
            tails = jnp.zeros((16, 128), F32)
            for i in range(4):
                q = 4 * j + i
                t = hw[w, 16 * c + q, :, pl.ds(128, 128)].astype(F32)
                tails = jnp.where(lane // 32 == i, pltpu.roll(t, 32 * i, 1) if i else t, tails)
                squares = jnp.where(
                    lane // 4 == q, pltpu.roll(t, (4 * q - 32) % 128, 1) if q != 8 else t, squares
                )
            ht[w, c, j] = tails.astype(BF16)
        ht[w, c, 4] = squares.astype(BF16)

    def w_copies(kind, c):
        step = (1, 7, 2, 6, 1, 7, 2, 6)[kind]
        at = lax.rem(w + (0, 0, 0, 0, 6, 2, 6, 2)[kind], 8)
        to = line_dev(step)
        slot_ = min(kind, 6) * 4 + c * 2
        main = hw.at[at, pl.ds(16 * c, 16), :, pl.ds(0, 128)]
        rest = ht.at[at, c]
        return [
            send(main, main, wl_s.at[slot_], wl_r.at[slot_], to),
            send(rest, rest, wl_s.at[slot_ + 1], wl_r.at[slot_ + 1], to),
        ]

    sent = []

    def w_send(kind, c):
        for cp in w_copies(kind, c):
            cp.start()
            sent.append(cp)

    def w_wait(kind, c):
        for cp in w_copies(kind, c):
            cp.wait_recv()

    for c in range(2):
        for kind in (2, 3):
            w_send(kind, c)
    for c in range(2):
        for kind in (0, 1):
            w_send(kind, c)

    for dz in (2, 6, 3, 5, 4):
        x_forward(dz)
    for c in range(2):
        for kind in (2, 3):
            w_wait(kind, c)
            w_send(kind + 2, c)
            if kind - 2 == c:
                w_send(kind + 4, c)

    acc[...] = jnp.zeros_like(acc)
    for cp in c_emb:
        cp.wait_recv()

    def slot(y2, x2, z2):
        return jnp.where(first, z2, y2), x2 * 8 + jnp.where(first, y2, z2)

    def add_product(lhs, e, s, n):
        for c in range(2):
            rhs = e[c, pl.ds(s, n)].reshape(256, COLS)
            acc[c] += jnp.dot(lhs, rhs, preferred_element_type=F32)

    def x_part(h2):
        def go(p, carry):
            cols = []
            for k in range(2):
                cols.append(
                    jnp.concatenate([hx[2 * h2 + b % 2, (2 * p + k) * 8 + b // 2] for b in range(16)], axis=0)
                )
            add_product(jnp.concatenate(cols, axis=1), e0, h2 * 8 + 2 * p, 2)
            return carry
        return go

    def w_part(h2):
        def go(p, carry):
            cols = []
            for k in range(2):
                tiles = []
                for b in range(16):
                    w2, p2 = slot(b // 2, 2 * h2 + b % 2, 2 * p + k)
                    tiles.append(hw[w2, p2, :, pl.ds(0, 128)])
                cols.append(jnp.concatenate(tiles, axis=0))
            add_product(jnp.concatenate(cols, axis=1), e1, h2 * 8 + 2 * p, 2)
            return carry
        return go

    def x_wait(k):
        def go(z2, carry):
            x_copy(k, z2).wait_recv()
            return carry
        lax.fori_loop(0, 8, go, 0)

    x_wait(1)
    lax.fori_loop(0, 4, x_part(xh), 0)
    x_wait(2)
    x_wait(3)
    lax.fori_loop(0, 4, x_part(1 - xh), 0)
    for c in range(2):
        for kind in (0, 1, 4, 5, 6):
            w_wait(kind, c)
        lax.fori_loop(0, 4, w_part(c), 0)

    @pl.when(first)
    def _():
        for h2 in range(2):
            for xl2 in range(2):
                for yq in range(2):
                    for zg in range(2):
                        src = [ht[4 * zg + i, h2, xl2 * 2 + yq].astype(F32) for i in range(4)]
                        for yi in range(4):
                            t = src[0]
                            for i in range(4):
                                by = 32 * ((i - yi) % 4)
                                moved = pltpu.roll(src[i], by, 1) if by else src[i]
                                t = jnp.where(lane // 32 == i, moved, t)
                            b = 2 * (4 * yq + yi) + xl2
                            lt_buf[pl.ds(16 * b, 16), pl.ds(128 * (2 * h2 + zg), 128)] = t.astype(BF16)

    @pl.when(jnp.logical_not(first))
    def _():
        for h2 in range(2):
            for b in range(16):
                for zg in range(2):
                    lt_buf[pl.ds(16 * b, 16), pl.ds(128 * (2 * h2 + zg), 128)] = ht[b // 2, h2, (b % 2) * 2 + zg]

    for h2 in range(2):
        add_product(lt_buf[:, pl.ds(256 * h2, 256)], e2, 8 * h2, 8)

    both = [ht[w2, 0, 4].astype(F32) + ht[w2, 1, 4].astype(F32) for w2 in range(8)]
    everything = both[0]
    for w2 in range(1, 8):
        everything = everything + both[w2]
    key = jnp.where(first, lane // 4, lane // 32)
    for b in range(16):
        t = jnp.where(first, everything, both[b // 2])
        mine = key == jnp.where(first, (b % 2) * 8 + b // 2, b % 2)
        t = jnp.sum(jnp.where(mine, t, 0.0), axis=1, keepdims=True)
        scale_buf[pl.ds(16 * b, 16), :] = jnp.broadcast_to(lax.rsqrt(t / D_ALL + 1e-06), (16, 128))
    own_scale = scale_buf[pl.ds(pl.multiple_of(16 * (2 * y + xl), 16), 16), pl.ds(0, 1)]
    fh_out[...] = (m_buf[:, pl.ds(0, WID)] * own_scale * g_row).astype(BF16)

    scale = scale_buf[:, pl.ds(0, 1)]
    lt = jnp.concatenate([(acc[c] * scale).T for c in range(2)], axis=0)
    top = jnp.max(lt, axis=0, keepdims=True)
    lse = top + jnp.log(jnp.sum(jnp.exp(lt - top), axis=0, keepdims=True))
    lane4 = lax.broadcasted_iota(jnp.int32, (4, 128), 1)
    lane1 = lax.broadcasted_iota(jnp.int32, (1, 128), 1)
    ids4 = t_in[...]
    ids4 = jnp.where(first, ids4, pltpu.roll(ids4, 112, 1))
    half = jnp.zeros((4, 128), jnp.int32)
    for m in range(4):
        moved = ids4 if m == 0 else pltpu.roll(ids4, 128 - 16 * m, 1)
        half = jnp.where(lane4 // 16 == m, moved, half)
    far = pltpu.roll(half, 64, 1)
    own_ids = jnp.concatenate(
        [jnp.where(lane1 < 64, half[2 * r : 2 * r + 1], far[2 * r + 1 : 2 * r + 2]) for r in range(2)], axis=1
    )
    ids = lax.broadcasted_iota(jnp.int32, (2 * COLS, 256), 0) + (sec * 32 + tp - core) * COLS
    tgt = jnp.sum(jnp.where(ids == own_ids, lt, 0.0), axis=0, keepdims=True)

    def put(ref, lse, tgt):
        ref[0:1, :] = lse[:, 0:128]
        ref[1:2, :] = lse[:, 128:256]
        ref[2:3, :] = tgt[:, 0:128]
        ref[3:4, :] = tgt[:, 128:256]

    def merge(ref, n):
        ls = ref[:, 0:2, :]
        top = jnp.max(ls, axis=0)
        return top + jnp.log(jnp.sum(jnp.exp(ls - top[None]), axis=0)), jnp.sum(ref[:, 2:4, :], axis=0)

    put(st1.at[w], lse, tgt)

    def s1_copy(i):
        return send(st1.at[w], st1.at[w], s1_s.at[i], s1_r.at[i], line_dev(i))

    def s2_copy(i):
        return send(st2.at[x * 8 + u], st2.at[x * 8 + u], s2_s.at[i], s2_r.at[i], plane_dev(i))

    lax.fori_loop(1, 8, starter(s1_copy), 0)
    lax.fori_loop(1, 8, waiter(s1_copy), 0)
    ls1, tg1 = merge(st1, 8)
    st2[x * 8 + u, 0:2, :] = ls1
    st2[x * 8 + u, 2:4, :] = tg1
    lax.fori_loop(1, 32, starter(s2_copy), 0)
    lax.fori_loop(1, 32, waiter(s2_copy), 0)
    ls2, tg2 = merge(st2, 32)
    lp = tg2 - ls2
    turned = pltpu.roll(lp, 64, 1)
    rows4 = jnp.concatenate([lp[0:1], turned[0:1], lp[1:2], turned[1:2]], axis=0)
    wide = jnp.zeros((4, 128), F32)
    for m in range(4):
        moved = rows4 if m == 0 else pltpu.roll(rows4, 16 * m, 1)
        wide = jnp.where(lane4 // 16 == 2 * m, moved, wide)
    res[core] = jnp.where(first, wide, pltpu.roll(wide, 16, 1))
    c_res = send(res.at[core], res.at[core], core_s.at[4], core_r.at[4], sibling)
    c_res.start()

    c_pair.wait_send()
    for cp in c_emb:
        cp.wait_send()
    lax.fori_loop(1, 16, ender(rs_copy), 0)
    lax.fori_loop(1, 32, ender(wp_copy), 0)
    lax.fori_loop(1, 64, ender(xp_copy), 0)
    for k in (1, 2, 3):
        def x_end(z2, carry, k=k):
            x_copy(k, z2).wait_send()
            return carry
        lax.fori_loop(0, 8, x_end, 0)
    for cp in sent:
        cp.wait_send()
    lax.fori_loop(1, 8, ender(s1_copy), 0)
    lax.fori_loop(1, 32, ender(s2_copy), 0)
    c_res.wait()
    lp_out[...] = res[0] + res[1]


def hand_on(fh, lp, fh_out, lp_out, sem):
    a = pltpu.make_async_copy(fh, fh_out, sem.at[0])
    b = pltpu.make_async_copy(lp, lp_out, sem.at[1])
    a.start()
    b.start()
    a.wait()
    b.wait()


def body(resid, act, w_down, gain, embed, targets):
    anyspec = pl.BlockSpec(memory_space=pl.ANY)
    vmem = pl.BlockSpec(memory_space=pltpu.VMEM)
    dma = pltpu.SemaphoreType.DMA
    fh, lp = pl.pallas_call(
        kernel,
        out_shape=(
            jax.ShapeDtypeStruct((16, WID), BF16),
            jax.ShapeDtypeStruct((4, 128), F32),
        ),
        in_specs=[anyspec] * 6,
        out_specs=(vmem, vmem),
        scratch_shapes=[
            pltpu.VMEM((2, 16, 16, HID), BF16),
            pltpu.VMEM((WID, HID), BF16),
            pltpu.VMEM((16, WID), BF16),
            pltpu.VMEM((WID,), F32),
            pltpu.VMEM((4, 128), jnp.int32),
            pltpu.VMEM((2, 16, 128, COLS), BF16),
            pltpu.VMEM((2, 16, 128, COLS), BF16),
            pltpu.VMEM((2, 16, 32, COLS), BF16),
            pltpu.VMEM((256, PADW), F32),
            pltpu.VMEM((256, PADW), F32),
            pltpu.VMEM((256, PADW), F32),
            pltpu.VMEM((16, 5, 8, 128), F32),
            pltpu.VMEM((16, 5, 8, 128), F32),
            pltpu.VMEM((16, PADW), F32),
            pltpu.VMEM((4, 64, 16, 128), BF16),
            pltpu.VMEM((8, 32, 16, 256), BF16),
            pltpu.VMEM((8, 2, 5, 16, 128), BF16),
            pltpu.VMEM((256, 512), BF16),
            pltpu.VMEM((256, 128), F32),
            pltpu.VMEM((2, 256, COLS), F32),
            pltpu.VMEM((8, 4, 128), F32),
            pltpu.VMEM((32, 4, 128), F32),
            pltpu.VMEM((2, 4, 128), F32),
            dma((9,)), dma((5,)), dma((5,)), dma((16,)), dma((16,)), dma((64,)), dma((64,)), dma((32,)), dma((32,)),
            dma((32,)), dma((32,)), dma((28,)), dma((28,)), dma((8,)), dma((8,)), dma((32,)), dma((32,)),
        ],
        compiler_params=pltpu.CompilerParams(
            collective_id=0, has_side_effects=True, vmem_limit_bytes=60 << 20
        ),
        name="ffn_vocab",
    )(
        act.reshape(16, 2, 16, HID),
        w_down.T,
        resid,
        gain,
        embed.reshape(16, WID, COLS),
        targets.reshape(4, 128),
    )
    fh, lp = pl.pallas_call(
        hand_on,
        out_shape=(
            jax.ShapeDtypeStruct((16, WID), BF16),
            jax.ShapeDtypeStruct((4, 128), F32),
        ),
        in_specs=[anyspec] * 2,
        out_specs=(anyspec, anyspec),
        scratch_shapes=[dma((2,))],
        name="hand_on",
    )(fh, lp)
    return fh, lp.reshape(512)


def solution(mesh):
    return jax.shard_map(
        body,
        mesh=mesh,
        in_specs=(
            P("tp", "section"),
            P(None, "tp"),
            P("tp", "section"),
            P("section"),
            P(None, ("section", "tp")),
            P(),
        ),
        out_specs=(P("tp", "section"), P()),
        check_vma=False,
    )
```

time: 90 us -> 77.1 us (0.86)
  local copies, waits for them, and re-layouts: 7.63 us -> 0 us
  Pallas kernels: 81.3 us -> 76.3 us
    pallas_call x1, Pallas kernels: 81.3 us -> 74.8 us  [body(): pl.pallas_call(kernel, out_shape=(jax.ShapeDtypeStruct((16, WID), BF16),...]
    unnamed x9 -> x0, local copies, waits for them, and re-layouts: 5.33 us -> none
    reshape x6 -> x0, local copies, waits for them, and re-layouts: 2.29 us -> none  [the longest x2 0.85 us: body(): targets.reshape(16, 2, 16).transpose(1, 0, 2).reshape(2, 1, 256)]
    pallas_call x0 -> x1, Pallas kernels: none -> 1.56 us  [body(): pl.pallas_call(hand_on, out_shape=(jax.ShapeDtypeStruct((16, WID), BF16),...]
where the time goes in v2:
time: 77.1 us; the launch traced here: 77 us
  Pallas kernels  76.3 us (99%)
    pallas_call x1, Pallas kernels, body(): pl.pallas_call(kernel, out_shape=(jax.ShapeDtypeStruct((16, WID), BF16),...  74.8 us
    pallas_call x1, Pallas kernels, body(): pl.pallas_call(hand_on, out_shape=(jax.ShapeDtypeStruct((16, WID), BF16),...  1.56 us

profile of v2, /device:TPU:1, one launch (start us, length us, event | category | flops | bytes accessed | tf_op | source)
XLA Modules:
  0.0 77.0 jit_solution(14585843828242100748)
XLA Ops:
  0.6 74.8 %ffn_vocab.1 = (bf16[16,288]{1,0:T(8,128)(2,1)}, f32[4,128]{1,0:T(4,128)}) custom-call(bf16[16,2,16,1152]{3,2,1,0:T(8,128)(2,1)} %bitcast.6, bf16[288,1152]{1,0:T(8,128)(2,1)} %bitcast.7, bf16[16,288]{1,0:T(8,128)(2,1)} %resid.1, f32[288]{0:T(512)} %gain.1, bf16[16,288,256]{2,1,0:T(8,128)(2,1)} %bitcast.5, s32[4,128]{1,0:T(4,128)} %bitcast.8), custom_call_target="tpu_custom_call" | custom-call | tf_op jit(solution)/shard_map/ffn_vocab/pallas_call | solution.py:460
  75.4 1.6 %hand_on.1 = (bf16[16,288]{1,0:T(8,128)(2,1)}, f32[4,128]{1,0:T(4,128)}) custom-call(bf16[16,288]{1,0:T(8,128)(2,1)} %get-tuple-element.6.fh, f32[4,128]{1,0:T(4,128)} %get-tuple-element.7.lp), custom_call_target="tpu_custom_call" | custom-call | tf_op jit(solution)/shard_map/hand_on/pallas_call | solution.py:507

commit v3 on v2

--- a/solution.py
+++ b/solution.py
@@ -58,8 +58,8 @@
     def plane_dev(i):
         return grid_dev(lax.rem(x + i // 8, 4), lax.rem(u + i, 8), w)
 
-    def yz_dev(i):
-        return dev(x, lax.rem(y + i // 8, 8), lax.rem(z + i, 8), core)
+    def u_dev(i):
+        return grid_dev(x, lax.rem(u + i, 8), w)
 
     def x_dev(k):
         return dev(2 * lax.rem(xh + k // 2, 2) + lax.rem(xl + k, 2), y, z, core)
@@ -92,8 +92,8 @@
         return go
 
     lax.fori_loop(0, 8, sig(lambda i: rs_dev(2 * i + 1)), 0)
-    lax.fori_loop(1, 64, sig(yz_dev), 0)
-    lax.fori_loop(8, 32, sig(plane_dev), 0)
+    lax.fori_loop(1, 8, sig(line_dev), 0)
+    lax.fori_loop(1, 32, sig(plane_dev), 0)
 
     p_out[:, pl.ds(256, 128)] = jnp.zeros((256, 128), F32)
     p_own[:, pl.ds(256, 128)] = jnp.zeros((256, 128), F32)
@@ -106,7 +106,7 @@
     l_w.wait()
     l_a0.wait()
     p_out[:, pl.ds(0, WID)] = partial(0)
-    pl.semaphore_wait(barrier, 1 + 8 + 63 + 24)
+    pl.semaphore_wait(barrier, 1 + 8 + 7 + 31)
     c_pair = send(p_out, p_in, core_s.at[0], core_r.at[0], sibling)
     c_pair.start()
     l_a1.wait()
@@ -129,7 +129,8 @@
         rs_copy(i).start()
         return carry
 
-    lax.fori_loop(1, 16, rs_start, 0)
+    for i in (8, 9, 6, 7, 10, 11, 4, 5, 12, 13, 2, 3, 14, 15, 1):
+        rs_copy(i).start()
 
     l_e.wait()
     l_f.wait()
@@ -173,7 +174,7 @@
     w_own = hw.at[w, x * 8 + u]
     w_own[:, pl.ds(128, 128)] = tail.astype(BF16)
     w_own[:, pl.ds(0, 160)] = piece[:, 128:288]
-    hx[x, z * 8 + y] = piece[:, 0:128]
+    hx[x, w * 8 + u] = piece[:, 0:128]
 
     def starter(copy):
         def go(i, carry):
@@ -197,31 +198,34 @@
         at = hw.at[w, x * 8 + u]
         return send(at, at, wp_s.at[i], wp_r.at[i], plane_dev(i))
 
-    def xp_copy(i):
-        at = hx.at[x, z * 8 + y]
-        return send(at, at, xp_s.at[i], xp_r.at[i], yz_dev(i))
-
-    def x_copy(k, z2):
-        block = hx.at[x, pl.ds(pl.multiple_of(z2 * 8, 8), 8)]
-        return send(block, block, xl_s.at[k * 8 + z2], xl_r.at[k * 8 + z2], x_dev(k))
-
-    def x_forward(dz):
-        def go(i, carry):
-            xp_copy(8 * i + dz).wait_recv()
-            return carry
-        lax.fori_loop(0 if dz else 1, 8, go, 0)
-        z2 = lax.rem(z + 8 - dz, 8)
+    def xu_copy(i):
+        at = hx.at[x, w * 8 + u]
+        return send(at, at, xp_s.at[i], xp_r.at[i], u_dev(i))
+
+    def chunk(w2):
+        return hx.at[x, pl.ds(pl.multiple_of(w2 * 8, 8), 8)]
+
+    def xw_copy(j):
+        return send(chunk(w), chunk(w), xp_s.at[8 + j], xp_r.at[8 + j], line_dev(j))
+
+    def x_copy(k, w2):
+        return send(chunk(w2), chunk(w2), xl_s.at[k * 8 + w2], xl_r.at[k * 8 + w2], x_dev(k))
+
+    def x_forward(j):
+        xw_copy(j).wait_recv()
         for k in (1, 2, 3):
-            x_copy(k, z2).start()
-
-    lax.fori_loop(1, 32, starter(wp_copy), 0)
-    for dz in (0, 1, 7, 2, 6, 3, 5, 4):
-        def go(i, carry, dz=dz):
-            xp_copy(8 * i + dz).start()
-            return carry
-        lax.fori_loop(0 if dz else 1, 8, go, 0)
-    for dz in (0, 1, 7):
-        x_forward(dz)
+            x_copy(k, lax.rem(w + 8 - j, 8)).start()
+
+    lax.fori_loop(1, 8, starter(xu_copy), 0)
+    for du in (4, 3, 5, 2, 6, 1, 7, 0):
+        for dx in (2, 1, 3, 0):
+            if du or dx:
+                wp_copy(8 * dx + du).start()
+    lax.fori_loop(1, 8, waiter(xu_copy), 0)
+    for j in (4, 3, 5, 2, 6, 1, 7):
+        xw_copy(j).start()
+    for k in (1, 2, 3):
+        x_copy(k, w).start()
     lax.fori_loop(1, 32, waiter(wp_copy), 0)
 
     for c in range(2):
@@ -268,8 +272,8 @@
         for kind in (0, 1):
             w_send(kind, c)
 
-    for dz in (2, 6, 3, 5, 4):
-        x_forward(dz)
+    for j in (1, 7, 2, 6, 3, 5, 4):
+        x_forward(j)
     for c in range(2):
         for kind in (2, 3):
             w_wait(kind, c)
@@ -284,6 +288,9 @@
     def slot(y2, x2, z2):
         return jnp.where(first, z2, y2), x2 * 8 + jnp.where(first, y2, z2)
 
+    def place(y2, z2):
+        return jnp.where(first, z2 * 8 + y2, y2 * 8 + z2)
+
     def add_product(lhs, e, s, n):
         for c in range(2):
             rhs = e[c, pl.ds(s, n)].reshape(256, COLS)
@@ -294,7 +301,7 @@
             cols = []
             for k in range(2):
                 cols.append(
-                    jnp.concatenate([hx[2 * h2 + b % 2, (2 * p + k) * 8 + b // 2] for b in range(16)], axis=0)
+                    jnp.concatenate([hx[2 * h2 + b % 2, place(b // 2, 2 * p + k)] for b in range(16)], axis=0)
                 )
             add_product(jnp.concatenate(cols, axis=1), e0, h2 * 8 + 2 * p, 2)
             return carry
@@ -430,7 +437,8 @@
         cp.wait_send()
     lax.fori_loop(1, 16, ender(rs_copy), 0)
     lax.fori_loop(1, 32, ender(wp_copy), 0)
-    lax.fori_loop(1, 64, ender(xp_copy), 0)
+    lax.fori_loop(1, 8, ender(xu_copy), 0)
+    lax.fori_loop(1, 8, ender(xw_copy), 0)
     for k in (1, 2, 3):
         def x_end(z2, carry, k=k):
             x_copy(k, z2).wait_send()
@@ -489,7 +497,7 @@
             pltpu.VMEM((8, 4, 128), F32),
             pltpu.VMEM((32, 4, 128), F32),
             pltpu.VMEM((2, 4, 128), F32),
-            dma((9,)), dma((5,)), dma((5,)), dma((16,)), dma((16,)), dma((64,)), dma((64,)), dma((32,)), dma((32,)),
+            dma((9,)), dma((5,)), dma((5,)), dma((16,)), dma((16,)), dma((16,)), dma((16,)), dma((32,)), dma((32,)),
             dma((32,)), dma((32,)), dma((28,)), dma((28,)), dma((8,)), dma((8,)), dma((32,)), dma((32,)),
         ],
         compiler_params=pltpu.CompilerParams(

time: 77.1 us -> 72 us (0.934)
  Pallas kernels: 76.3 us -> 71.2 us
    pallas_call x1, Pallas kernels: 74.8 us -> 69.6 us  [body(): pl.pallas_call(kernel, out_shape=(jax.ShapeDtypeStruct((16, WID), BF16),...]
where the time goes in v3:
time: 72 us; the launch traced here: 71.8 us
  Pallas kernels  71.2 us (99%)
    pallas_call x1, Pallas kernels, body(): pl.pallas_call(kernel, out_shape=(jax.ShapeDtypeStruct((16, WID), BF16),...  69.6 us
    pallas_call x1, Pallas kernels, body(): pl.pallas_call(hand_on, out_shape=(jax.ShapeDtypeStruct((16, WID), BF16),...  1.56 us

profile of v3, /device:TPU:1, one launch (start us, length us, event | category | flops | bytes accessed | tf_op | source)
XLA Modules:
  0.0 71.8 jit_solution(135421200499798525)
XLA Ops:
  0.6 69.6 %ffn_vocab.1 = (bf16[16,288]{1,0:T(8,128)(2,1)}, f32[4,128]{1,0:T(4,128)}) custom-call(bf16[16,2,16,1152]{3,2,1,0:T(8,128)(2,1)} %bitcast.6, bf16[288,1152]{1,0:T(8,128)(2,1)} %bitcast.7, bf16[16,288]{1,0:T(8,128)(2,1)} %resid.1, f32[288]{0:T(512)} %gain.1, bf16[16,288,256]{2,1,0:T(8,128)(2,1)} %bitcast.5, s32[4,128]{1,0:T(4,128)} %bitcast.8), custom_call_target="tpu_custom_call" | custom-call | tf_op jit(solution)/shard_map/ffn_vocab/pallas_call | solution.py:468
  70.3 1.6 %hand_on.1 = (bf16[16,288]{1,0:T(8,128)(2,1)}, f32[4,128]{1,0:T(4,128)}) custom-call(bf16[16,288]{1,0:T(8,128)(2,1)} %get-tuple-element.6.fh, f32[4,128]{1,0:T(4,128)} %get-tuple-element.7.lp), custom_call_target="tpu_custom_call" | custom-call | tf_op jit(solution)/shard_map/hand_on/pallas_call | solution.py:515

commit v4 on v3

--- a/solution.py
+++ b/solution.py
@@ -213,7 +213,7 @@
 
     def x_forward(j):
         xw_copy(j).wait_recv()
-        for k in (1, 2, 3):
+        for k in (2, 1, 3):
             x_copy(k, lax.rem(w + 8 - j, 8)).start()
 
     lax.fori_loop(1, 8, starter(xu_copy), 0)
@@ -224,7 +224,7 @@
     lax.fori_loop(1, 8, waiter(xu_copy), 0)
     for j in (4, 3, 5, 2, 6, 1, 7):
         xw_copy(j).start()
-    for k in (1, 2, 3):
+    for k in (2, 1, 3):
         x_copy(k, w).start()
     lax.fori_loop(1, 32, waiter(wp_copy), 0)
 
@@ -266,10 +266,7 @@
             cp.wait_recv()
 
     for c in range(2):
-        for kind in (2, 3):
-            w_send(kind, c)
-    for c in range(2):
-        for kind in (0, 1):
+        for kind in (2, 3, 0, 1):
             w_send(kind, c)
 
     for j in (1, 7, 2, 6, 3, 5, 4):
@@ -373,7 +370,6 @@
         t = jnp.sum(jnp.where(mine, t, 0.0), axis=1, keepdims=True)
         scale_buf[pl.ds(16 * b, 16), :] = jnp.broadcast_to(lax.rsqrt(t / D_ALL + 1e-06), (16, 128))
     own_scale = scale_buf[pl.ds(pl.multiple_of(16 * (2 * y + xl), 16), 16), pl.ds(0, 1)]
-    fh_out[...] = (m_buf[:, pl.ds(0, WID)] * own_scale * g_row).astype(BF16)
 
     scale = scale_buf[:, pl.ds(0, 1)]
     lt = jnp.concatenate([(acc[c] * scale).T for c in range(2)], axis=0)
@@ -413,12 +409,17 @@
     def s2_copy(i):
         return send(st2.at[x * 8 + u], st2.at[x * 8 + u], s2_s.at[i], s2_r.at[i], plane_dev(i))
 
-    lax.fori_loop(1, 8, starter(s1_copy), 0)
+    for i in (4, 3, 5, 2, 6, 1, 7):
+        s1_copy(i).start()
+    fh_out[...] = (m_buf[:, pl.ds(0, WID)] * own_scale * g_row).astype(BF16)
     lax.fori_loop(1, 8, waiter(s1_copy), 0)
     ls1, tg1 = merge(st1, 8)
     st2[x * 8 + u, 0:2, :] = ls1
     st2[x * 8 + u, 2:4, :] = tg1
-    lax.fori_loop(1, 32, starter(s2_copy), 0)
+    for du in (4, 3, 5, 2, 6, 1, 7, 0):
+        for dx in (2, 1, 3, 0):
+            if du or dx:
+                s2_copy(8 * dx + du).start()
     lax.fori_loop(1, 32, waiter(s2_copy), 0)
     ls2, tg2 = merge(st2, 32)
     lp = tg2 - ls2
@@ -452,13 +453,9 @@
     lp_out[...] = res[0] + res[1]
 
 
-def hand_on(fh, lp, fh_out, lp_out, sem):
-    a = pltpu.make_async_copy(fh, fh_out, sem.at[0])
-    b = pltpu.make_async_copy(lp, lp_out, sem.at[1])
-    a.start()
-    b.start()
-    a.wait()
-    b.wait()
+def hand_on(fh, lp, fh_out, lp_out):
+    fh_out[...] = fh[...]
+    lp_out[...] = lp[...]
 
 
 def body(resid, act, w_down, gain, embed, targets):
@@ -518,9 +515,8 @@
             jax.ShapeDtypeStruct((16, WID), BF16),
             jax.ShapeDtypeStruct((4, 128), F32),
         ),
-        in_specs=[anyspec] * 2,
-        out_specs=(anyspec, anyspec),
-        scratch_shapes=[dma((2,))],
+        in_specs=[vmem] * 2,
+        out_specs=(vmem, vmem),
         name="hand_on",
     )(fh, lp)
     return fh, lp.reshape(512)

time: 72 us -> 71.1 us (0.987)
  Pallas kernels: 71.2 us -> 70.3 us
where the time goes in v4:
time: 71.1 us; the launch traced here: 70.9 us
  Pallas kernels  70.3 us (99%)
    pallas_call x1, Pallas kernels, body(): pl.pallas_call(kernel, out_shape=(jax.ShapeDtypeStruct((16, WID), BF16),...  69 us

profile of v4, /device:TPU:1, one launch (start us, length us, event | category | flops | bytes accessed | tf_op | source)
XLA Modules:
  0.0 70.9 jit_solution(503661814899046465)
XLA Ops:
  0.6 69.0 %ffn_vocab.1 = (bf16[16,288]{1,0:T(8,128)(2,1)}, f32[4,128]{1,0:T(4,128)}) custom-call(bf16[16,2,16,1152]{3,2,1,0:T(8,128)(2,1)} %bitcast.6, bf16[288,1152]{1,0:T(8,128)(2,1)} %bitcast.7, bf16[16,288]{1,0:T(8,128)(2,1)} %resid.1, f32[288]{0:T(512)} %gain.1, bf16[16,288,256]{2,1,0:T(8,128)(2,1)} %bitcast.5, s32[4,128]{1,0:T(4,128)} %bitcast.8), custom_call_target="tpu_custom_call" | custom-call | tf_op jit(solution)/shard_map/ffn_vocab/pallas_call | solution.py:465
  69.6 1.3 %hand_on.1 = (bf16[16,288]{1,0:T(8,128)(2,1)}, f32[4,128]{1,0:T(4,128)}) custom-call(bf16[16,288]{1,0:T(8,128)(2,1)} %get-tuple-element.6.fh, f32[4,128]{1,0:T(4,128)} %get-tuple-element.7.lp), custom_call_target="tpu_custom_call" | custom-call | tf_op jit(solution)/shard_map/hand_on/pallas_call | solution.py:512

commit v5 on v4

--- a/solution.py
+++ b/solution.py
@@ -112,8 +112,9 @@
     l_a1.wait()
     p_own[:, pl.ds(0, WID)] = partial(1)
     c_pair.wait_recv()
-    for b in range(16):
-        rows = pl.ds(16 * b, 16)
+
+    def pack(b):
+        rows = pl.ds(pl.multiple_of(16 * b, 16), 16)
         v = p_own[rows, :] + p_in[rows, :]
         s_buf[b, 0] = v[0:8, 0:128]
         s_buf[b, 1] = v[0:8, 128:256]
@@ -130,7 +131,10 @@
         return carry
 
     for i in (8, 9, 6, 7, 10, 11, 4, 5, 12, 13, 2, 3, 14, 15, 1):
+        y2, xl2 = rs_peer(i)
+        pack(y2 * 2 + xl2)
         rs_copy(i).start()
+    pack(y * 2 + xl)
 
     l_e.wait()
     l_f.wait()

time: 71.1 us -> 71.6 us (level)
  no operation moved by 1% of the time
where the time goes in v5:
time: 71.6 us; the launch traced here: 71.4 us
  Pallas kernels  70.7 us (99%)
    pallas_call x1, Pallas kernels, body(): pl.pallas_call(kernel, out_shape=(jax.ShapeDtypeStruct((16, WID), BF16),...  69.4 us

profile of v5, /device:TPU:1, one launch (start us, length us, event | category | flops | bytes accessed | tf_op | source)
XLA Modules:
  0.0 71.4 jit_solution(10844161031705329280)
XLA Ops:
  0.6 69.4 %ffn_vocab.1 = (bf16[16,288]{1,0:T(8,128)(2,1)}, f32[4,128]{1,0:T(4,128)}) custom-call(bf16[16,2,16,1152]{3,2,1,0:T(8,128)(2,1)} %bitcast.6, bf16[288,1152]{1,0:T(8,128)(2,1)} %bitcast.7, bf16[16,288]{1,0:T(8,128)(2,1)} %resid.1, f32[288]{0:T(512)} %gain.1, bf16[16,288,256]{2,1,0:T(8,128)(2,1)} %bitcast.5, s32[4,128]{1,0:T(4,128)} %bitcast.8), custom_call_target="tpu_custom_call" | custom-call | tf_op jit(solution)/shard_map/ffn_vocab/pallas_call | solution.py:469
  70.0 1.3 %hand_on.1 = (bf16[16,288]{1,0:T(8,128)(2,1)}, f32[4,128]{1,0:T(4,128)}) custom-call(bf16[16,288]{1,0:T(8,128)(2,1)} %get-tuple-element.6.fh, f32[4,128]{1,0:T(4,128)} %get-tuple-element.7.lp), custom_call_target="tpu_custom_call" | custom-call | tf_op jit(solution)/shard_map/hand_on/pallas_call | solution.py:516
